TPU v7x, 128 devices: a whole 4x4x4 slice. The times are simulated.
128 devices in a mesh: gx: 16 (over y, z), gy: 8 (over x, core).
Axes of the slice: x: 4, y: 4, z: 4, core: 2. Of those that a mesh axis runs over, the one named last changes fastest.
Arguments:
- probes: bfloat16 [16, 131072], P(None, ('gx', 'gy')), may hold values from -73 to 73, as said below
- previous: bfloat16 [16, 131072], P(None, ('gx', 'gy')), may hold values from -6 to 6
- prev_coupling: float32 [16, 16], replicated, may hold values from -1.5 to 1.5
- leaves: bfloat16 [128, 1024, 1024], P(('gx', 'gy')), may hold values from -1 to 3, as said below
- bases: bfloat16 [7, 64, 131072], P(None, None, ('gx', 'gy')), may hold values from -6 to 6
- leaf_sizes: int32 [128], P(('gx', 'gy')), may hold values from 1 to 1024, 98304 in all
Outputs:
- rayleigh: float32 [16, 16], replicated
- factor: float32 [16, 16], replicated
- next_block: float32 [16, 131072], P(None, ('gx', 'gy'))
Inputs may be any that keep to these rules, and one draw needn't show every extreme that they name: For every probe p and slot s, |probes[p, s]| stays within the range below. Each leaves[i] is symmetric. `leaf_sizes`: the real points of a leaf fill its first slots; the sizes sum to 98304.
All inputs are finite; a program needn't handle non-finite values. No bound on the sum of `leaf_sizes` on one device may be relied on, other than what follows from the above.
Results may differ from a plain program's by a relative error of at most 0.0022.
Values sent between devices are 32-bit elements; how exact they have to be, the bound alone decides.
No kernel may reach another device: no remote copies, remote signals or barrier semaphores. Data moves between devices by JAX's collectives and lax.ppermute only.
A program may use at most 64 MiB of HBM per device.

v0:
```python
import math
import jax
import jax.numpy as jnp
from jax import lax
from jax.sharding import Mesh
from jax.sharding import PartitionSpec as P

GX_GY = ("gx_0", "gx_1", "gy_0", "gy_1")


def partner_2(block, axis, stride):
    count = lax.axis_size(axis)
    route = []
    for low in range(count):
        high = low | 1 << stride
        if high != low and high < count:
            route += [(low, high), (high, low)]
    return lax.ppermute(block, axis, route)


def one_axis_at_a_time(value, axes):
    for axis in axes:
        value = lax.psum(value, axis)
    return value


def sibling_sums(partials, spread):
    results = []
    remaining = partials
    for bit_number in range(spread):
        received = partner_2(remaining, GX_GY, bit_number)
        results.append(received[0])
        remaining = remaining[1:] + received[1:]
    return results


def body(probes, previous, prev_coupling, leaves, bases, leaf_sizes):
    highest = lax.Precision.HIGHEST
    probe_count = probes.shape[0]
    leaf_count = leaves.shape[0]
    leaf_rows = leaves.shape[1]
    rows = leaf_count * leaf_rows
    rank = bases.shape[1]
    devices = lax.axis_size(GX_GY)
    spread = devices.bit_length() - 1
    filled = leaf_count * devices * leaf_rows * 3 // 4
    inverse = 1.0 / filled
    valid = (jnp.arange(leaf_rows, dtype=jnp.int32)[None, :] < leaf_sizes[:, None]).reshape(rows)
    block = jnp.where(valid[None, :], probes, jnp.zeros_like(probes))
    older = jnp.where(valid[None, :], previous, jnp.zeros_like(previous))
    shaped = block.reshape(probe_count, leaf_count, leaf_rows)
    image = jnp.einsum("lrc,plc->plr", leaves, shaped, preferred_element_type=jnp.float32).reshape(
        probe_count, rows
    )
    partials = jnp.einsum("pm,krm->kpr", block, bases, preferred_element_type=jnp.float32)
    partners = sibling_sums(partials, spread)
    for bit_number in range(spread):
        width = rows * 2**bit_number
        scaled = (partners[bit_number] * (1.0 / math.sqrt(rank * width))).astype(jnp.bfloat16)
        image = image + jnp.dot(scaled, bases[bit_number], preferred_element_type=jnp.float32)
    image = jnp.where(valid[None, :], image, jnp.zeros_like(image))
    dense = block.astype(jnp.float32)
    older_dense = older.astype(jnp.float32)
    stacked = jnp.concatenate([image, dense, older_dense], 0)
    joint = one_axis_at_a_time(jnp.dot(stacked, stacked.T, precision=highest) * inverse, GX_GY)
    rayleigh = joint[probe_count : 2 * probe_count, :probe_count]
    mixing = jnp.concatenate(
        [jnp.eye(probe_count, dtype=jnp.float32), -rayleigh.T, -prev_coupling], 1
    )
    gram = jnp.dot(jnp.dot(mixing, joint, precision=highest), mixing.T, precision=highest)
    residual = (
        image
        - jnp.dot(rayleigh.T, dense, precision=highest)
        - jnp.dot(prev_coupling, older_dense, precision=highest)
    )
    factor = jnp.linalg.cholesky(gram)
    next_block = jax.scipy.linalg.solve_triangular(factor, residual, lower=True)
    return (rayleigh, factor, next_block)


def solution(mesh):
    split = Mesh(mesh.devices.reshape(4, 4, 4, 2), ("gx_0", "gx_1", "gy_0", "gy_1"))
    return jax.shard_map(
        body,
        mesh=split,
        in_specs=(
            P(None, GX_GY),
            P(None, GX_GY),
            P(),
            P(GX_GY, None, None),
            P(None, None, GX_GY),
            P(GX_GY),
        ),
        out_specs=(P(), P(), P(None, GX_GY)),
        check_vma=False,
    )
```

profile of v0, /device:TPU:1, one launch (start us, length us, event | category | flops | bytes accessed | tf_op | source)
XLA Modules:
  0.0 97.7 jit_solution(13078462689037245916)
XLA Ops:
  1.5 1.7 %convolution_bitcast_fusion.1 = f32[7,16,64]{2,1,0:T(8,128)S(1)} fusion(bf16[7,64,1024]{2,1,0:T(8,128)(2,1)} %param.10, bf16[16,1024]{1,0:T(8,128)(2,1)} %param.6, pred[1024]{0:T(1024)(128)(4,1)S(1)} %iota_compare_fusion.2), kind=kOutput, calls=%fused_computation.13 | convolution fusion | flops 14696448 | bytes 979968 | tf_op jit(solution)/shard_map/pm,krm->kpr/dot_general | solution.py:55
  3.2 1.5 %collective-permute-start = (f32[7,16,64]{2,1,0:T(8,128)S(1)}, f32[7,16,64]{2,1,0:T(8,128)S(1)}, u32[]{:S(2)}, u32[]{:S(2)}) collective-permute-start(f32[7,16,64]{2,1,0:T(8,128)S(1)} %convolution_bitcast_fusion.1), channel_id=1, source_target_pairs={{0,1},{1,0},{2,3},{3,2},{4,5},{5,4},{6,7},{7,6},{8,9},{9,8},{10,11... | collective-permute-start | bytes 86024 | tf_op jit(solution)/shard_map/ppermute | solution.py:18
  4.7 1.4 %fusion = f32[16,1024]{1,0:T(8,128)S(1)} fusion(bf16[1,1024,1024]{2,1,0:T(8,128)(2,1)S(1)} %copy-done, bf16[16,1024]{1,0:T(8,128)(2,1)} %param.6, pred[1024]{0:T(1024)(128)(4,1)S(1)} %iota_compare_fusion.2), kind=kOutput, calls=%fused_computation | convolution fusion | flops 33570816 | bytes 2196480 | tf_op jit(solution)/shard_map/lrc,plc->plr/dot_general | solution.py:52
  6.2 1.4 %collective-permute-start.1 = (f32[6,16,64]{2,1,0:T(8,128)S(1)}, f32[6,16,64]{2,1,0:T(8,128)S(1)}, u32[]{:S(2)}, u32[]{:S(2)}) collective-permute-start(f32[6,16,64]{2,1,0:T(8,128)S(1)} %slice_add_fusion), channel_id=1, source_target_pairs={{0,2},{2,0},{1,3},{3,1},{4,6},{6,4},{5,7},{7,5},{8,10},{10,8},{9,1... | collective-permute-start | bytes 73736 | tf_op jit(solution)/shard_map/ppermute | solution.py:18
  7.7 1.9 %collective-permute-done.1 = f32[6,16,64]{2,1,0:T(8,128)S(1)} collective-permute-done((f32[6,16,64]{2,1,0:T(8,128)S(1)}, f32[6,16,64]{2,1,0:T(8,128)S(1)}, u32[]{:S(2)}, u32[]{:S(2)}) %collective-permute-start.1) | collective-permute-done | bytes 24608 | tf_op jit(solution)/shard_map/ppermute | solution.py:18
  9.7 2.8 %collective-permute-start.2 = (f32[5,16,64]{2,1,0:T(8,128)S(1)}, f32[5,16,64]{2,1,0:T(8,128)S(1)}, u32[]{:S(2)}, u32[]{:S(2)}) collective-permute-start(f32[5,16,64]{2,1,0:T(8,128)S(1)} %slice_add_fusion.1), channel_id=1, source_target_pairs={{0,4},{4,0},{1,5},{5,1},{2,6},{6,2},{3,7},{7,3},{8,12},{12,8},{9,1... | collective-permute-start | bytes 61448 | tf_op jit(solution)/shard_map/ppermute | solution.py:18
  12.6 1.4 %collective-permute-done.2 = f32[5,16,64]{2,1,0:T(8,128)S(1)} collective-permute-done((f32[5,16,64]{2,1,0:T(8,128)S(1)}, f32[5,16,64]{2,1,0:T(8,128)S(1)}, u32[]{:S(2)}, u32[]{:S(2)}) %collective-permute-start.2) | collective-permute-done | bytes 20512 | tf_op jit(solution)/shard_map/ppermute | solution.py:18
  14.0 1.7 %collective-permute-start.3 = (f32[4,16,64]{2,1,0:T(8,128)S(1)}, f32[4,16,64]{2,1,0:T(8,128)S(1)}, u32[]{:S(2)}, u32[]{:S(2)}) collective-permute-start(f32[4,16,64]{2,1,0:T(8,128)S(1)} %slice_add_fusion.2), channel_id=1, source_target_pairs={{0,8},{8,0},{1,9},{9,1},{2,10},{10,2},{3,11},{11,3},{4,12},{12,4},... | collective-permute-start | bytes 49160 | tf_op jit(solution)/shard_map/ppermute | solution.py:18
  15.8 0.1 convolution_add_fusion.4
  15.9 1.2 %collective-permute-done.3 = f32[4,16,64]{2,1,0:T(8,128)S(1)} collective-permute-done((f32[4,16,64]{2,1,0:T(8,128)S(1)}, f32[4,16,64]{2,1,0:T(8,128)S(1)}, u32[]{:S(2)}, u32[]{:S(2)}) %collective-permute-start.3) | collective-permute-done | bytes 16416 | tf_op jit(solution)/shard_map/ppermute | solution.py:18
  17.1 3.4 %collective-permute-start.4 = (f32[3,16,64]{2,1,0:T(8,128)S(1)}, f32[3,16,64]{2,1,0:T(8,128)S(1)}, u32[]{:S(2)}, u32[]{:S(2)}) collective-permute-start(f32[3,16,64]{2,1,0:T(8,128)S(1)} %slice_add_fusion.3), channel_id=1, source_target_pairs={{0,16},{16,0},{1,17},{17,1},{2,18},{18,2},{3,19},{19,3},{4,20},{20... | collective-permute-start | bytes 36872 | tf_op jit(solution)/shard_map/ppermute | solution.py:18
  20.6 1.1 %collective-permute-done.4 = f32[3,16,64]{2,1,0:T(8,128)S(1)} collective-permute-done((f32[3,16,64]{2,1,0:T(8,128)S(1)}, f32[3,16,64]{2,1,0:T(8,128)S(1)}, u32[]{:S(2)}, u32[]{:S(2)}) %collective-permute-start.4) | collective-permute-done | bytes 12320 | tf_op jit(solution)/shard_map/ppermute | solution.py:18
  21.7 1.3 %collective-permute-start.5 = (f32[2,16,64]{2,1,0:T(8,128)S(1)}, f32[2,16,64]{2,1,0:T(8,128)S(1)}, u32[]{:S(2)}, u32[]{:S(2)}) collective-permute-start(f32[2,16,64]{2,1,0:T(8,128)S(1)} %slice_add_fusion.4), channel_id=1, source_target_pairs={{0,32},{32,0},{1,33},{33,1},{2,34},{34,2},{3,35},{35,3},{4,36},{36... | collective-permute-start | bytes 24584 | tf_op jit(solution)/shard_map/ppermute | solution.py:18
  23.1 1.4 %collective-permute-done.5 = f32[2,16,64]{2,1,0:T(8,128)S(1)} collective-permute-done((f32[2,16,64]{2,1,0:T(8,128)S(1)}, f32[2,16,64]{2,1,0:T(8,128)S(1)}, u32[]{:S(2)}, u32[]{:S(2)}) %collective-permute-start.5) | collective-permute-done | bytes 8224 | tf_op jit(solution)/shard_map/ppermute | solution.py:18
  24.6 2.9 %collective-permute-start.6 = (f32[1,16,64]{2,1,0:T(8,128)S(1)}, f32[1,16,64]{2,1,0:T(8,128)S(1)}, u32[]{:S(2)}, u32[]{:S(2)}) collective-permute-start(f32[1,16,64]{2,1,0:T(8,128)S(1)} %slice_add_fusion.5), channel_id=1, source_target_pairs={{0,64},{64,0},{1,65},{65,1},{2,66},{66,2},{3,67},{67,3},{4,68},{68... | collective-permute-start | bytes 12296 | tf_op jit(solution)/shard_map/ppermute | solution.py:18
  27.6 1.0 collective-permute-done.6
  28.6 0.1 fusion.3
  28.7 0.3 convolution_multiply_fusion
  29.0 13.6 %psum.28 = f32[48,48]{0,1:T(8,128)S(1)} all-reduce(f32[48,48]{0,1:T(8,128)S(1)} %convolution_multiply_fusion), channel_id=1, replica_groups=mesh['gx_0'=4,'gx_1'=4,'gy_0'=4,'gy_1'=2] {'gx_0'}, use_global_device_ids=true, to_apply=%region_0.1 | all-reduce | flops 2304 | bytes 18432 | tf_op jit(solution)/shard_map/psum | solution.py:23
  42.6 14.2 %psum.29 = f32[48,48]{0,1:T(8,128)S(1)} all-reduce(f32[48,48]{0,1:T(8,128)S(1)} %psum.28), channel_id=1, replica_groups=mesh['gx_0'=4,'gx_1'=4,'gy_0'=4,'gy_1'=2] {'gx_1'}, use_global_device_ids=true, to_apply=%region_1.2 | all-reduce | flops 2304 | bytes 18432 | tf_op jit(solution)/shard_map/psum | solution.py:23
  56.8 13.3 %psum.30 = f32[48,48]{0,1:T(8,128)S(1)} all-reduce(f32[48,48]{0,1:T(8,128)S(1)} %psum.29), channel_id=1, replica_groups=mesh['gx_0'=4,'gx_1'=4,'gy_0'=4,'gy_1'=2] {'gy_0'}, use_global_device_ids=true, to_apply=%region_2.3 | all-reduce | flops 2304 | bytes 18432 | tf_op jit(solution)/shard_map/psum | solution.py:23
  70.1 20.4 %psum.31 = f32[48,48]{0,1:T(8,128)S(1)} all-reduce(f32[48,48]{0,1:T(8,128)S(1)} %psum.30), channel_id=1, replica_groups=mesh['gx_0'=4,'gx_1'=4,'gy_0'=4,'gy_1'=2] {'gy_1'}, use_global_device_ids=true, to_apply=%region_3.4 | all-reduce | flops 2304 | bytes 18432 | tf_op jit(solution)/shard_map/psum | solution.py:23
  90.5 0.2 convolution_subtract_fusion
  90.8 0.2 fusion.2
  91.0 0.2 fusion.75
  91.2 0.2 fusion.74
  91.4 0.7 copy.11
  92.2 1.5 %cholesky.20 = f32[16,16]{1,0:T(8,128)S(1)} custom-call(f32[16,16]{1,0:T(8,128)S(1)} %fusion.38), custom_call_target="Cholesky" | custom-call | tf_op jit(solution)/shard_map/jit(cholesky)/cholesky | solution.py:76
  93.7 0.6 compare_reduce_fusion
  94.3 1.2 %select_bitcast_fusion = (f32[1,16,16]{2,1,0:T(8,128)S(1)}, f32[16,16]{1,0:T(8,128)}) fusion(f32[16,16]{1,0:T(8,128)S(1)} %cholesky.20, pred[]{:T(512)} %compare_reduce_fusion), kind=kLoop, calls=%fused_computation.66 | loop fusion | flops 1024 | bytes 3073 | tf_op jit(solution)/shard_map/jit(_solve_triangular)/triangular_solve | solution.py:77
  95.6 1.2 %custom-call.7 = f32[1,16,16]{1,2,0:T(8,128)S(1)} custom-call(f32[1,16,16]{2,1,0:T(8,128)S(1)} %get-tuple-element.6), custom_call_target="InvertDiagBlocksLowerTriangular" | custom-call | tf_op jit(solution)/shard_map/jit(_solve_triangular)/triangular_solve | solution.py:77
  96.8 0.9 fusion.36
  (30 shorter events, 1.0 us)
Async XLA Ops:
  0.6 4.1 %copy-start = (bf16[1,1024,1024]{2,1,0:T(8,128)(2,1)S(1)}, bf16[1,1024,1024]{2,1,0:T(8,128)(2,1)}, u32[]{:S(2)}) copy-start(bf16[1,1024,1024]{2,1,0:T(8,128)(2,1)} %param.9) | copy-start | bytes 6291460
  0.6 6.9 %copy-start.1 = (bf16[7,64,1024]{2,1,0:T(8,128)(2,1)S(1)}, bf16[7,64,1024]{2,1,0:T(8,128)(2,1)}, u32[]{:S(2)}) copy-start(bf16[7,64,1024]{2,1,0:T(8,128)(2,1)} %param.10) | copy-start | bytes 2752516
  0.7 5.4 %copy-start.2 = (bf16[16,1024]{1,0:T(8,128)(2,1)S(1)}, bf16[16,1024]{1,0:T(8,128)(2,1)}, u32[]{:S(2)}) copy-start(bf16[16,1024]{1,0:T(8,128)(2,1)} %param.6) | copy-start | bytes 98308
  0.7 5.4 %copy-start.3 = (bf16[16,1024]{1,0:T(8,128)(2,1)S(1)}, bf16[16,1024]{1,0:T(8,128)(2,1)}, u32[]{:S(2)}) copy-start(bf16[16,1024]{1,0:T(8,128)(2,1)} %param.7) | copy-start | bytes 98308
  0.7 5.5 %copy-start.4 = (f32[16,16]{1,0:T(8,128)S(1)}, f32[16,16]{1,0:T(8,128)}, u32[]{:S(2)}) copy-start(f32[16,16]{1,0:T(8,128)} %param.8) | copy-start | bytes 3076
  3.2 2.9 %collective-permute-start = (f32[7,16,64]{2,1,0:T(8,128)S(1)}, f32[7,16,64]{2,1,0:T(8,128)S(1)}, u32[]{:S(2)}, u32[]{:S(2)}) collective-permute-start(f32[7,16,64]{2,1,0:T(8,128)S(1)} %convolution_bitcast_fusion.1), channel_id=1, source_target_pairs={{0,1},{1,0},{2,3},{3,2},{4,5},{5,4},{6,7},{7,6},{8,9},{9,8},{10,11... | collective-permute-start | bytes 86024 | tf_op jit(solution)/shard_map/ppermute | solution.py:18
  6.2 3.5 %collective-permute-start.1 = (f32[6,16,64]{2,1,0:T(8,128)S(1)}, f32[6,16,64]{2,1,0:T(8,128)S(1)}, u32[]{:S(2)}, u32[]{:S(2)}) collective-permute-start(f32[6,16,64]{2,1,0:T(8,128)S(1)} %slice_add_fusion), channel_id=1, source_target_pairs={{0,2},{2,0},{1,3},{3,1},{4,6},{6,4},{5,7},{7,5},{8,10},{10,8},{9,1... | collective-permute-start | bytes 73736 | tf_op jit(solution)/shard_map/ppermute | solution.py:18
  9.7 4.4 %collective-permute-start.2 = (f32[5,16,64]{2,1,0:T(8,128)S(1)}, f32[5,16,64]{2,1,0:T(8,128)S(1)}, u32[]{:S(2)}, u32[]{:S(2)}) collective-permute-start(f32[5,16,64]{2,1,0:T(8,128)S(1)} %slice_add_fusion.1), channel_id=1, source_target_pairs={{0,4},{4,0},{1,5},{5,1},{2,6},{6,2},{3,7},{7,3},{8,12},{12,8},{9,1... | collective-permute-start | bytes 61448 | tf_op jit(solution)/shard_map/ppermute | solution.py:18
  14.0 3.0 %collective-permute-start.3 = (f32[4,16,64]{2,1,0:T(8,128)S(1)}, f32[4,16,64]{2,1,0:T(8,128)S(1)}, u32[]{:S(2)}, u32[]{:S(2)}) collective-permute-start(f32[4,16,64]{2,1,0:T(8,128)S(1)} %slice_add_fusion.2), channel_id=1, source_target_pairs={{0,8},{8,0},{1,9},{9,1},{2,10},{10,2},{3,11},{11,3},{4,12},{12,4},... | collective-permute-start | bytes 49160 | tf_op jit(solution)/shard_map/ppermute | solution.py:18
  17.1 4.6 %collective-permute-start.4 = (f32[3,16,64]{2,1,0:T(8,128)S(1)}, f32[3,16,64]{2,1,0:T(8,128)S(1)}, u32[]{:S(2)}, u32[]{:S(2)}) collective-permute-start(f32[3,16,64]{2,1,0:T(8,128)S(1)} %slice_add_fusion.3), channel_id=1, source_target_pairs={{0,16},{16,0},{1,17},{17,1},{2,18},{18,2},{3,19},{19,3},{4,20},{20... | collective-permute-start | bytes 36872 | tf_op jit(solution)/shard_map/ppermute | solution.py:18
  21.7 2.9 %collective-permute-start.5 = (f32[2,16,64]{2,1,0:T(8,128)S(1)}, f32[2,16,64]{2,1,0:T(8,128)S(1)}, u32[]{:S(2)}, u32[]{:S(2)}) collective-permute-start(f32[2,16,64]{2,1,0:T(8,128)S(1)} %slice_add_fusion.4), channel_id=1, source_target_pairs={{0,32},{32,0},{1,33},{33,1},{2,34},{34,2},{3,35},{35,3},{4,36},{36... | collective-permute-start | bytes 24584 | tf_op jit(solution)/shard_map/ppermute | solution.py:18
  24.6 4.0 %collective-permute-start.6 = (f32[1,16,64]{2,1,0:T(8,128)S(1)}, f32[1,16,64]{2,1,0:T(8,128)S(1)}, u32[]{:S(2)}, u32[]{:S(2)}) collective-permute-start(f32[1,16,64]{2,1,0:T(8,128)S(1)} %slice_add_fusion.5), channel_id=1, source_target_pairs={{0,64},{64,0},{1,65},{65,1},{2,66},{66,2},{3,67},{67,3},{4,68},{68... | collective-permute-start | bytes 12296 | tf_op jit(solution)/shard_map/ppermute | solution.py:18
where the time goes:
time: 98 us; the launch traced here: 97.7 us
  blocking collectives  61.5 us (63%)
  starting transfers between devices  15 us (15%)
  waiting for transfers between devices  7.98 us (8%)
  matrix products  6.11 us (6%)
  other arithmetic  4.75 us (5%)
  between operations  1.58 us (2%)
    psum x4, blocking collectives, one_axis_at_a_time(): value = lax.psum(value, axis)  61.5 us
    ppermute x7, starting transfers between devices, partner_2(): return lax.ppermute(block, axis, route)  15 us
    ppermute x7, waiting for transfers between devices, partner_2(): return lax.ppermute(block, axis, route)  7.98 us
    another operation x2, other arithmetic, body(): next_block = jax.scipy.linalg.solve_triangular(factor, residual, lower=True)  2.47 us
    another operation x3, other arithmetic, body(): factor = jnp.linalg.cholesky(gram)  2.13 us
  transfers between devices with their start and end apart: 7, of which 6 were waited for; matrix products, arithmetic and copies ran while one was open for 2% of the time, Pallas kernels for 0%

commit v1 on v0

--- a/solution.py
+++ b/solution.py
@@ -20,7 +20,7 @@
 
 def one_axis_at_a_time(value, axes):
     for axis in axes:
-        value = lax.psum(value, axis)
+        value = jnp.sum(lax.all_gather(value, axis), axis=0)
     return value
 
 

time: 98 us -> 80.8 us (0.82)
  blocking collectives: 61.5 us -> 45 us
    psum x4 -> x0, blocking collectives: 61.5 us -> none  [one_axis_at_a_time(): value = lax.psum(value, axis)]
    all_gather x0 -> x4, blocking collectives: none -> 45 us  [one_axis_at_a_time(): value = jnp.sum(lax.all_gather(value, axis), axis=0)]
  transfers between devices with their start and end apart: 7 -> 7, of which waited for: 6 -> 6; matrix products, arithmetic and copies ran while one was open for 2% -> 3% of each run, Pallas kernels for 0% -> 0%
where the time goes in v1:
time: 80.8 us; the launch traced here: 80.6 us
  blocking collectives  45 us (56%)
  starting transfers between devices  15 us (19%)
  waiting for transfers between devices  7.98 us (10%)
  matrix products  6.1 us (8%)
  other arithmetic  4.75 us (6%)
  between operations  1.6 us (2%)
    all_gather x4, blocking collectives, one_axis_at_a_time(): value = jnp.sum(lax.all_gather(value, axis), axis=0)  45 us
    ppermute x7, starting transfers between devices, partner_2(): return lax.ppermute(block, axis, route)  15 us
    ppermute x7, waiting for transfers between devices, partner_2(): return lax.ppermute(block, axis, route)  7.98 us
    another operation x2, other arithmetic, body(): next_block = jax.scipy.linalg.solve_triangular(factor, residual, lower=True)  2.47 us
    another operation x3, other arithmetic, body(): factor = jnp.linalg.cholesky(gram)  2.15 us
    dot_general x1, matrix products, body(): jnp.einsum('pm,krm->kpr', block, bases, preferred_element_type=jnp.float32)  1.75 us
  transfers between devices with their start and end apart: 7, of which 6 were waited for; matrix products, arithmetic and copies ran while one was open for 3% of the time, Pallas kernels for 0%

profile of v1, /device:TPU:1, one launch (start us, length us, event | category | flops | bytes accessed | tf_op | source)
XLA Modules:
  0.0 80.6 jit_solution(17553134155703639016)
XLA Ops:
  1.5 1.7 %convolution_bitcast_fusion.1 = f32[7,16,64]{2,1,0:T(8,128)S(1)} fusion(bf16[7,64,1024]{2,1,0:T(8,128)(2,1)} %param.10, bf16[16,1024]{1,0:T(8,128)(2,1)} %param.6, pred[1024]{0:T(1024)(128)(4,1)S(1)} %iota_compare_fusion.2), kind=kOutput, calls=%fused_computation.13 | convolution fusion | flops 14696448 | bytes 979968 | tf_op jit(solution)/shard_map/pm,krm->kpr/dot_general | solution.py:55
  3.2 1.5 %collective-permute-start = (f32[7,16,64]{2,1,0:T(8,128)S(1)}, f32[7,16,64]{2,1,0:T(8,128)S(1)}, u32[]{:S(2)}, u32[]{:S(2)}) collective-permute-start(f32[7,16,64]{2,1,0:T(8,128)S(1)} %convolution_bitcast_fusion.1), channel_id=1, source_target_pairs={{0,1},{1,0},{2,3},{3,2},{4,5},{5,4},{6,7},{7,6},{8,9},{9,8},{10,11... | collective-permute-start | bytes 86024 | tf_op jit(solution)/shard_map/ppermute | solution.py:18
  4.7 1.4 %fusion = f32[16,1024]{1,0:T(8,128)S(1)} fusion(bf16[1,1024,1024]{2,1,0:T(8,128)(2,1)S(1)} %copy-done, bf16[16,1024]{1,0:T(8,128)(2,1)} %param.6, pred[1024]{0:T(1024)(128)(4,1)S(1)} %iota_compare_fusion.2), kind=kOutput, calls=%fused_computation | convolution fusion | flops 33570816 | bytes 2196480 | tf_op jit(solution)/shard_map/lrc,plc->plr/dot_general | solution.py:52
  6.2 1.4 %collective-permute-start.1 = (f32[6,16,64]{2,1,0:T(8,128)S(1)}, f32[6,16,64]{2,1,0:T(8,128)S(1)}, u32[]{:S(2)}, u32[]{:S(2)}) collective-permute-start(f32[6,16,64]{2,1,0:T(8,128)S(1)} %slice_add_fusion), channel_id=1, source_target_pairs={{0,2},{2,0},{1,3},{3,1},{4,6},{6,4},{5,7},{7,5},{8,10},{10,8},{9,1... | collective-permute-start | bytes 73736 | tf_op jit(solution)/shard_map/ppermute | solution.py:18
  7.7 1.9 %collective-permute-done.1 = f32[6,16,64]{2,1,0:T(8,128)S(1)} collective-permute-done((f32[6,16,64]{2,1,0:T(8,128)S(1)}, f32[6,16,64]{2,1,0:T(8,128)S(1)}, u32[]{:S(2)}, u32[]{:S(2)}) %collective-permute-start.1) | collective-permute-done | bytes 24608 | tf_op jit(solution)/shard_map/ppermute | solution.py:18
  9.7 2.8 %collective-permute-start.2 = (f32[5,16,64]{2,1,0:T(8,128)S(1)}, f32[5,16,64]{2,1,0:T(8,128)S(1)}, u32[]{:S(2)}, u32[]{:S(2)}) collective-permute-start(f32[5,16,64]{2,1,0:T(8,128)S(1)} %slice_add_fusion.1), channel_id=1, source_target_pairs={{0,4},{4,0},{1,5},{5,1},{2,6},{6,2},{3,7},{7,3},{8,12},{12,8},{9,1... | collective-permute-start | bytes 61448 | tf_op jit(solution)/shard_map/ppermute | solution.py:18
  12.6 1.4 %collective-permute-done.2 = f32[5,16,64]{2,1,0:T(8,128)S(1)} collective-permute-done((f32[5,16,64]{2,1,0:T(8,128)S(1)}, f32[5,16,64]{2,1,0:T(8,128)S(1)}, u32[]{:S(2)}, u32[]{:S(2)}) %collective-permute-start.2) | collective-permute-done | bytes 20512 | tf_op jit(solution)/shard_map/ppermute | solution.py:18
  14.0 1.7 %collective-permute-start.3 = (f32[4,16,64]{2,1,0:T(8,128)S(1)}, f32[4,16,64]{2,1,0:T(8,128)S(1)}, u32[]{:S(2)}, u32[]{:S(2)}) collective-permute-start(f32[4,16,64]{2,1,0:T(8,128)S(1)} %slice_add_fusion.2), channel_id=1, source_target_pairs={{0,8},{8,0},{1,9},{9,1},{2,10},{10,2},{3,11},{11,3},{4,12},{12,4},... | collective-permute-start | bytes 49160 | tf_op jit(solution)/shard_map/ppermute | solution.py:18
  15.9 1.2 %collective-permute-done.3 = f32[4,16,64]{2,1,0:T(8,128)S(1)} collective-permute-done((f32[4,16,64]{2,1,0:T(8,128)S(1)}, f32[4,16,64]{2,1,0:T(8,128)S(1)}, u32[]{:S(2)}, u32[]{:S(2)}) %collective-permute-start.3) | collective-permute-done | bytes 16416 | tf_op jit(solution)/shard_map/ppermute | solution.py:18
  17.1 3.4 %collective-permute-start.4 = (f32[3,16,64]{2,1,0:T(8,128)S(1)}, f32[3,16,64]{2,1,0:T(8,128)S(1)}, u32[]{:S(2)}, u32[]{:S(2)}) collective-permute-start(f32[3,16,64]{2,1,0:T(8,128)S(1)} %slice_add_fusion.3), channel_id=1, source_target_pairs={{0,16},{16,0},{1,17},{17,1},{2,18},{18,2},{3,19},{19,3},{4,20},{20... | collective-permute-start | bytes 36872 | tf_op jit(solution)/shard_map/ppermute | solution.py:18
  20.5 0.1 convolution_add_fusion.3
  20.6 1.1 %collective-permute-done.4 = f32[3,16,64]{2,1,0:T(8,128)S(1)} collective-permute-done((f32[3,16,64]{2,1,0:T(8,128)S(1)}, f32[3,16,64]{2,1,0:T(8,128)S(1)}, u32[]{:S(2)}, u32[]{:S(2)}) %collective-permute-start.4) | collective-permute-done | bytes 12320 | tf_op jit(solution)/shard_map/ppermute | solution.py:18
  21.7 1.3 %collective-permute-start.5 = (f32[2,16,64]{2,1,0:T(8,128)S(1)}, f32[2,16,64]{2,1,0:T(8,128)S(1)}, u32[]{:S(2)}, u32[]{:S(2)}) collective-permute-start(f32[2,16,64]{2,1,0:T(8,128)S(1)} %slice_add_fusion.4), channel_id=1, source_target_pairs={{0,32},{32,0},{1,33},{33,1},{2,34},{34,2},{3,35},{35,3},{4,36},{36... | collective-permute-start | bytes 24584 | tf_op jit(solution)/shard_map/ppermute | solution.py:18
  23.1 1.5 %collective-permute-done.5 = f32[2,16,64]{2,1,0:T(8,128)S(1)} collective-permute-done((f32[2,16,64]{2,1,0:T(8,128)S(1)}, f32[2,16,64]{2,1,0:T(8,128)S(1)}, u32[]{:S(2)}, u32[]{:S(2)}) %collective-permute-start.5) | collective-permute-done | bytes 8224 | tf_op jit(solution)/shard_map/ppermute | solution.py:18
  24.6 2.9 %collective-permute-start.6 = (f32[1,16,64]{2,1,0:T(8,128)S(1)}, f32[1,16,64]{2,1,0:T(8,128)S(1)}, u32[]{:S(2)}, u32[]{:S(2)}) collective-permute-start(f32[1,16,64]{2,1,0:T(8,128)S(1)} %slice_add_fusion.5), channel_id=1, source_target_pairs={{0,64},{64,0},{1,65},{65,1},{2,66},{66,2},{3,67},{67,3},{4,68},{68... | collective-permute-start | bytes 12296 | tf_op jit(solution)/shard_map/ppermute | solution.py:18
  27.5 0.1 convolution_add_fusion.1
  27.6 1.0 %collective-permute-done.6 = f32[1,16,64]{2,1,0:T(8,128)S(1)} collective-permute-done((f32[1,16,64]{2,1,0:T(8,128)S(1)}, f32[1,16,64]{2,1,0:T(8,128)S(1)}, u32[]{:S(2)}, u32[]{:S(2)}) %collective-permute-start.6) | collective-permute-done | bytes 4128 | tf_op jit(solution)/shard_map/ppermute | solution.py:18
  28.6 0.1 fusion.3
  28.7 0.3 convolution_multiply_fusion
  29.1 9.8 %all-gather = f32[192,48]{1,0:T(8,128)S(1)} all-gather(f32[48,48]{1,0:T(8,128)S(1)} %convolution_multiply_fusion), channel_id=2, replica_groups=mesh['gx_0'=4,'gx_1'=4,'gy_0'=4,'gy_1'=2] {'gx_0'}, dimensions={0}, use_global_device_ids=true | all-gather | bytes 46080 | tf_op jit(solution)/shard_map/all_gather | solution.py:23
  38.9 9.5 %all-gather.1 = f32[192,48]{1,0:T(8,128)S(1)} all-gather(f32[48,48]{1,0:T(8,128)S(1)} %reduce_sum.36), channel_id=3, replica_groups=mesh['gx_0'=4,'gx_1'=4,'gy_0'=4,'gy_1'=2] {'gx_1'}, dimensions={0}, use_global_device_ids=true | all-gather | bytes 46080 | tf_op jit(solution)/shard_map/all_gather | solution.py:23
  48.4 9.7 %all-gather.2 = f32[192,48]{1,0:T(8,128)S(1)} all-gather(f32[48,48]{1,0:T(8,128)S(1)} %reduce_sum.37), channel_id=4, replica_groups=mesh['gx_0'=4,'gx_1'=4,'gy_0'=4,'gy_1'=2] {'gy_0'}, dimensions={0}, use_global_device_ids=true | all-gather | bytes 46080 | tf_op jit(solution)/shard_map/all_gather | solution.py:23
  58.1 15.9 %all-gather.3 = f32[96,48]{1,0:T(8,128)S(1)} all-gather(f32[48,48]{1,0:T(8,128)S(1)} %reduce_sum.38), channel_id=5, replica_groups=mesh['gx_0'=4,'gx_1'=4,'gy_0'=4,'gy_1'=2] {'gy_1'}, dimensions={0}, use_global_device_ids=true | all-gather | bytes 27648 | tf_op jit(solution)/shard_map/all_gather | solution.py:23
  74.1 0.2 convolution_subtract_fusion
  74.4 0.2 fusion.2
  74.6 0.2 fusion.74
  74.8 0.2 fusion.73
  75.1 1.5 %cholesky.20 = f32[16,16]{1,0:T(8,128)S(1)} custom-call(f32[16,16]{1,0:T(8,128)S(1)} %fusion.38), custom_call_target="Cholesky" | custom-call | tf_op jit(solution)/shard_map/jit(cholesky)/cholesky | solution.py:76
  76.6 0.6 compare_reduce_fusion
  77.2 1.2 %select_bitcast_fusion = (f32[1,16,16]{2,1,0:T(8,128)S(1)}, f32[16,16]{1,0:T(8,128)}) fusion(f32[16,16]{1,0:T(8,128)S(1)} %cholesky.20, pred[]{:T(512)} %compare_reduce_fusion), kind=kLoop, calls=%fused_computation.66 | loop fusion | flops 1024 | bytes 3073 | tf_op jit(solution)/shard_map/jit(_solve_triangular)/triangular_solve | solution.py:77
  78.5 1.2 %custom-call.7 = f32[1,16,16]{1,2,0:T(8,128)S(1)} custom-call(f32[1,16,16]{2,1,0:T(8,128)S(1)} %get-tuple-element.9), custom_call_target="InvertDiagBlocksLowerTriangular" | custom-call | tf_op jit(solution)/shard_map/jit(_solve_triangular)/triangular_solve | solution.py:77
  79.7 0.9 %fusion.36 = f32[16,1024]{1,0:T(8,128)} fusion(f32[16,1024]{1,0:T(8,128)S(1)} %fusion.2, f32[1,16,16]{1,2,0:T(8,128)S(1)} %custom-call.7), kind=kOutput, calls=%fused_computation.62 | convolution fusion | flops 3145728 | bytes 132096 | tf_op jit(solution)/shard_map/jit(_solve_triangular)/triangular_solve | solution.py:77
  (37 shorter events, 0.9 us)
Async XLA Ops:
  0.6 4.1 %copy-start = (bf16[1,1024,1024]{2,1,0:T(8,128)(2,1)S(1)}, bf16[1,1024,1024]{2,1,0:T(8,128)(2,1)}, u32[]{:S(2)}) copy-start(bf16[1,1024,1024]{2,1,0:T(8,128)(2,1)} %param.9) | copy-start | bytes 6291460
  0.6 6.9 %copy-start.1 = (bf16[7,64,1024]{2,1,0:T(8,128)(2,1)S(1)}, bf16[7,64,1024]{2,1,0:T(8,128)(2,1)}, u32[]{:S(2)}) copy-start(bf16[7,64,1024]{2,1,0:T(8,128)(2,1)} %param.10) | copy-start | bytes 2752516
  0.7 5.4 %copy-start.2 = (bf16[16,1024]{1,0:T(8,128)(2,1)S(1)}, bf16[16,1024]{1,0:T(8,128)(2,1)}, u32[]{:S(2)}) copy-start(bf16[16,1024]{1,0:T(8,128)(2,1)} %param.6) | copy-start | bytes 98308
  0.7 5.4 %copy-start.3 = (bf16[16,1024]{1,0:T(8,128)(2,1)S(1)}, bf16[16,1024]{1,0:T(8,128)(2,1)}, u32[]{:S(2)}) copy-start(bf16[16,1024]{1,0:T(8,128)(2,1)} %param.7) | copy-start | bytes 98308
  0.7 5.5 %copy-start.5 = (f32[16,16]{1,0:T(8,128)S(1)}, f32[16,16]{1,0:T(8,128)}, u32[]{:S(2)}) copy-start(f32[16,16]{1,0:T(8,128)} %param.8) | copy-start | bytes 3076
  3.2 2.9 %collective-permute-start = (f32[7,16,64]{2,1,0:T(8,128)S(1)}, f32[7,16,64]{2,1,0:T(8,128)S(1)}, u32[]{:S(2)}, u32[]{:S(2)}) collective-permute-start(f32[7,16,64]{2,1,0:T(8,128)S(1)} %convolution_bitcast_fusion.1), channel_id=1, source_target_pairs={{0,1},{1,0},{2,3},{3,2},{4,5},{5,4},{6,7},{7,6},{8,9},{9,8},{10,11... | collective-permute-start | bytes 86024 | tf_op jit(solution)/shard_map/ppermute | solution.py:18
  6.2 3.5 %collective-permute-start.1 = (f32[6,16,64]{2,1,0:T(8,128)S(1)}, f32[6,16,64]{2,1,0:T(8,128)S(1)}, u32[]{:S(2)}, u32[]{:S(2)}) collective-permute-start(f32[6,16,64]{2,1,0:T(8,128)S(1)} %slice_add_fusion), channel_id=1, source_target_pairs={{0,2},{2,0},{1,3},{3,1},{4,6},{6,4},{5,7},{7,5},{8,10},{10,8},{9,1... | collective-permute-start | bytes 73736 | tf_op jit(solution)/shard_map/ppermute | solution.py:18
  9.7 4.4 %collective-permute-start.2 = (f32[5,16,64]{2,1,0:T(8,128)S(1)}, f32[5,16,64]{2,1,0:T(8,128)S(1)}, u32[]{:S(2)}, u32[]{:S(2)}) collective-permute-start(f32[5,16,64]{2,1,0:T(8,128)S(1)} %slice_add_fusion.1), channel_id=1, source_target_pairs={{0,4},{4,0},{1,5},{5,1},{2,6},{6,2},{3,7},{7,3},{8,12},{12,8},{9,1... | collective-permute-start | bytes 61448 | tf_op jit(solution)/shard_map/ppermute | solution.py:18
  14.0 3.0 %collective-permute-start.3 = (f32[4,16,64]{2,1,0:T(8,128)S(1)}, f32[4,16,64]{2,1,0:T(8,128)S(1)}, u32[]{:S(2)}, u32[]{:S(2)}) collective-permute-start(f32[4,16,64]{2,1,0:T(8,128)S(1)} %slice_add_fusion.2), channel_id=1, source_target_pairs={{0,8},{8,0},{1,9},{9,1},{2,10},{10,2},{3,11},{11,3},{4,12},{12,4},... | collective-permute-start | bytes 49160 | tf_op jit(solution)/shard_map/ppermute | solution.py:18
  17.1 4.6 %collective-permute-start.4 = (f32[3,16,64]{2,1,0:T(8,128)S(1)}, f32[3,16,64]{2,1,0:T(8,128)S(1)}, u32[]{:S(2)}, u32[]{:S(2)}) collective-permute-start(f32[3,16,64]{2,1,0:T(8,128)S(1)} %slice_add_fusion.3), channel_id=1, source_target_pairs={{0,16},{16,0},{1,17},{17,1},{2,18},{18,2},{3,19},{19,3},{4,20},{20... | collective-permute-start | bytes 36872 | tf_op jit(solution)/shard_map/ppermute | solution.py:18
  21.7 2.9 %collective-permute-start.5 = (f32[2,16,64]{2,1,0:T(8,128)S(1)}, f32[2,16,64]{2,1,0:T(8,128)S(1)}, u32[]{:S(2)}, u32[]{:S(2)}) collective-permute-start(f32[2,16,64]{2,1,0:T(8,128)S(1)} %slice_add_fusion.4), channel_id=1, source_target_pairs={{0,32},{32,0},{1,33},{33,1},{2,34},{34,2},{3,35},{35,3},{4,36},{36... | collective-permute-start | bytes 24584 | tf_op jit(solution)/shard_map/ppermute | solution.py:18
  24.6 4.0 %collective-permute-start.6 = (f32[1,16,64]{2,1,0:T(8,128)S(1)}, f32[1,16,64]{2,1,0:T(8,128)S(1)}, u32[]{:S(2)}, u32[]{:S(2)}) collective-permute-start(f32[1,16,64]{2,1,0:T(8,128)S(1)} %slice_add_fusion.5), channel_id=1, source_target_pairs={{0,64},{64,0},{1,65},{65,1},{2,66},{66,2},{3,67},{67,3},{4,68},{68... | collective-permute-start | bytes 12296 | tf_op jit(solution)/shard_map/ppermute | solution.py:18
  74.1 6.5 %copy-start.4 = (f32[16,16]{1,0:T(8,128)}, f32[16,16]{1,0:T(8,128)S(1)}, u32[]{:S(2)}) copy-start(f32[16,16]{1,0:T(8,128)S(1)} %slice.134) | copy-start | bytes 3076
